TPU v7x, 256 devices: a whole 4x4x8 slice. The times are simulated.
256 devices in a mesh: wide: 64 (over x, z, y_lo), loop: 4 (over y_hi, core).
Axes of the slice: x: 4, y: 4 (y_hi: 2, y_lo: 2; y = y_hi * 2 + y_lo), z: 8, core: 2. Of those that a mesh axis runs over, the one named last changes fastest.
Arguments:
- diag_block: float32 [512, 512], P('wide')
- panel: float32 [98304, 512], P('wide'), may hold values from -12 to 12
- trailing: float32 [98304, 4096], P('wide', 'loop'), may hold values from -6 to 6
- fill_mask: int32 [768, 32], P('wide', 'loop'), may hold values 0 or 1
- column_tiles: int32 [32], P('loop'), may hold values from 0 to 767
Outputs:
- updated: float32 [98304, 4096], P('wide', 'loop')
All inputs are finite; a program needn't handle non-finite values. No bound on the sum of `fill_mask` on one device may be relied on, other than what follows from the above.
Results may differ from a plain program's by a relative error of at most 0.00005.
Values sent between devices are 32-bit elements; how exact they have to be, the bound alone decides.
A program may use at most 128 MiB of HBM per device.

v0:
```python
import jax
import jax.numpy as jnp
from jax import lax
from jax.sharding import PartitionSpec as P


def solve_panel(rows_in, factor):
    return jax.scipy.linalg.solve_triangular(factor, rows_in.T, lower=True).T


def shards(diag_block, panel, trailing, fill_mask, column_tiles):
    precise = lax.Precision.HIGHEST
    gathered = lax.all_gather(diag_block, "wide", axis=0, tiled=True)
    factor = jnp.linalg.cholesky(gathered)
    rows_dev = panel.shape[0]
    panel_width = panel.shape[1]
    col_tiles = column_tiles.shape[0]
    tile_size = trailing.shape[1] // col_tiles
    part_rows = rows_dev // lax.axis_size("loop")
    own_rows = lax.dynamic_slice_in_dim(panel, lax.axis_index("loop") * part_rows, part_rows, 0)
    lower_panel = lax.all_gather(solve_panel(own_rows, factor), "loop", axis=0, tiled=True)
    tiles_dev = rows_dev // tile_size
    first_tile = lax.axis_index("wide") * tiles_dev
    owned_tiles = first_tile + jnp.arange(tiles_dev, dtype=jnp.int32)
    selector = (column_tiles[:, None] == owned_tiles[None, :]).astype(jnp.float32)
    tile_blocks = lower_panel.reshape(tiles_dev, tile_size * panel_width)
    local_pick = jnp.dot(selector, tile_blocks, precision=precise)
    picked = lax.psum(local_pick, "wide").reshape(col_tiles * tile_size, panel_width)
    update = lax.dot_general(lower_panel, picked, (((1,), (1,)), ((), ())), precision=precise)
    masked = (
        update.reshape(tiles_dev, tile_size, col_tiles, tile_size)
        * fill_mask.astype(jnp.float32)[:, None, :, None]
    )
    return trailing - masked.reshape(trailing.shape)


def solution(mesh):
    return jax.shard_map(
        shards,
        mesh=mesh,
        in_specs=(
            P("wide", None),
            P("wide", None),
            P("wide", "loop"),
            P("wide", "loop"),
            P("loop"),
        ),
        out_specs=P("wide", "loop"),
        check_vma=False,
    )
```

profile of v0, /device:TPU:16, one launch (start us, length us, event | category | flops | bytes accessed | tf_op | source)
XLA Modules:
  0.0 1168.3 jit_solution(18094251524899507940)
XLA Ops:
  11.7 297.2 %all-gather.3.cloned.1.call-done = f32[512,512]{1,0:T(8,128)} async-done(((f32[8,512]{1,0:T(8,128)}), f32[512,512]{1,0:T(8,128)}) %all-gather.3.cloned.1.call-update) | async-done | bytes 1048592 | tf_op jit(solution)/shard_map/all_gather | solution.py:13
  308.8 2.5 copy.18
  314.1 11.7 %cholesky.104 = f32[128,128]{1,0:T(8,128)S(1)} custom-call(f32[128,128]{1,0:T(8,128)S(1)} %cholesky.266), custom_call_target="Cholesky" | custom-call | tf_op jit(solution)/shard_map/jit(cholesky)/cholesky | solution.py:14
  325.9 9.8 custom-call.31
  340.0 11.7 %cholesky.217 = f32[128,128]{1,0:T(8,128)S(1)} custom-call(f32[128,128]{1,0:T(8,128)S(1)} %cholesky.270), custom_call_target="Cholesky" | custom-call | tf_op jit(solution)/shard_map/jit(cholesky)/cholesky | solution.py:14
  352.3 10.0 custom-call.32
  364.8 11.7 %cholesky.238 = f32[128,128]{1,0:T(8,128)S(1)} custom-call(f32[128,128]{1,0:T(8,128)S(1)} %cholesky.275), custom_call_target="Cholesky" | custom-call | tf_op jit(solution)/shard_map/jit(cholesky)/cholesky | solution.py:14
  377.8 9.8 custom-call.33
  389.8 24.1 %cholesky.255 = f32[128,128]{1,0:T(8,128)S(1)} custom-call(f32[128,128]{1,0:T(8,128)S(1)} %convolution_subtract_fusion.5), custom_call_target="Cholesky" | custom-call | tf_op jit(solution)/shard_map/jit(cholesky)/cholesky | solution.py:14
  420.8 14.1 %while.1 = (s32[]{:T(128)}, f32[512,512]{1,0:T(8,128)}, s32[4,2]{0,1:T(2,128)S(1)}, f32[4,128,128]{2,1,0:T(8,128)}, s32[]{:T(128)}) while((s32[]{:T(128)}, f32[512,512]{1,0:T(8,128)}, s32[4,2]{0,1:T(2,128)S(1)}, f32[4,128,128]{2,1,0:T(8,128)}, s32[]{:T(128)}) %tuple.27), condition=%wide.while_cond, body=%wide.while_body.sunk | while | flops 2 | bytes 132205 | solution.py:8
  421.5 2.9 bitcast_dynamic-update-slice_fusion.2
  425.0 2.9 bitcast_dynamic-update-slice_fusion.2
  428.6 2.9 bitcast_dynamic-update-slice_fusion.2
  432.1 2.8 bitcast_dynamic-update-slice_fusion.2
  434.9 40.1 %custom-call.34 = f32[4,128,128]{1,2,0:T(8,128)S(1)} custom-call(f32[4,128,128]{2,1,0:T(8,128)} %get-tuple-element.12), custom_call_target="InvertDiagBlocksLowerTriangular" | custom-call | tf_op jit(solution)/shard_map/jit(_solve_triangular)/triangular_solve | solution.py:8
  482.8 29.7 %all-gather.5.cloned.1.call-done = f32[1536,512]{0,1:T(8,128)} async-done(((f32[384,512]{0,1:T(8,128)}), f32[1536,512]{0,1:T(8,128)}) %all-gather.5.cloned.1.call-update) | async-done | bytes 3145744 | tf_op jit(solution)/shard_map/all_gather | solution.py:21
  512.5 3.5 copy.20
  516.0 4.0 reshape.56
  520.0 3.7 fusion.29
  523.8 2.5 copy.22
  526.4 611.6 %all-reduce.3.cloned.1.call-done = f32[8,128,512]{2,1,0:T(8,128)} async-done(((f32[8,128,512]{2,1,0:T(8,128)}), f32[8,128,512]{2,1,0:T(8,128)}) %all-reduce.3.cloned.1.call-update) | async-done | bytes 2097168 | tf_op jit(solution)/shard_map/psum | solution.py:28
  1138.0 13.9 %broadcast_multiply_fusion = f32[12,128,8,128]{3,1,2,0:T(8,128)S(1)} fusion(f32[12,8]{1,0:T(8,128)S(1)} %copy.23, f32[12,128,512,1]{2,1,3,0:T(8,128)} %bitcast.66, f32[8,128,512]{2,1,0:T(8,128)} %all-reduce.3.cloned.1.call-done), kind=kOutput, calls=%fused_computation.3 | convolution fusion | flops 9665249280 | bytes 11534720 | tf_op jit(solution)/shard_map/dot_general | solution.py:29
  1151.9 4.4 copy.24
  1156.3 5.0 bitcast_subtract_fusion
  (62 shorter events, 33.5 us)
Async XLA Ops:
  6.5 1.9 copy-start
  6.5 302.3 %all-gather.3.cloned.1.call-start = ((), (), s32[]{:S(2)}) async-start(), calls=%async_computation | async-start | bytes 1064960 | tf_op jit(solution)/shard_map/all_gather | solution.py:13
  7.3 505.2 %all-gather.5.cloned.1.call-start = ((), (), s32[]{:S(2)}) async-start(), calls=%async_computation.1 | async-start | bytes 3932160 | tf_op jit(solution)/shard_map/all_gather | solution.py:21
  313.1 1.0 copy-start.1
  482.7 655.3 %all-reduce.3.cloned.1.call-start = ((), (), s32[]{:S(2)}) async-start(), calls=%async_computation.2 | async-start | bytes 4194304 | tf_op jit(solution)/shard_map/psum | solution.py:28
  516.0 4.0 copy-start.3
  523.7 2.6 copy-start.2
  1138.0 18.3 %slice-start = ((s8[6291456]{0:T(1024)(128)(4,1)}), s8[4194304]{0:T(1024)(128)(4,1)S(1)}, s32[]{:S(2)}) async-start(s8[6291456]{0:T(1024)(128)(4,1)} %bitcast.69), calls=%async_computation.3 | async-start | bytes 8388608
  1151.9 4.4 slice-start.1
Sparse Core Ops, SparseCore 0:
  9.1 299.6 all-gather.2
  482.8 29.5 all-gather.4
  526.4 611.5 all-reduce.2
where the time goes:
time: 1180 us; the launch traced here: 1170 us
  waiting for transfers between devices  939 us (80%)
  other arithmetic  143 us (12%)
  local copies, waits for them, and re-layouts  37.7 us (3%)
  matrix products  32 us (3%)
  between operations  16.2 us (1%)
    psum x1, waiting for transfers between devices, shards(): lax.psum(local_pick, 'wide').reshape(col_tiles * tile_size, panel_width)  612 us
    all_gather x1, waiting for transfers between devices, shards(): gathered = lax.all_gather(diag_block, 'wide', axis=0, tiled=True)  297 us
    another operation x14, other arithmetic, shards(): factor = jnp.linalg.cholesky(gathered)  92.9 us
    another operation x3, other arithmetic, solve_panel(): return jax.scipy.linalg.solve_triangular(factor, rows_in.T, lower=True).T  42.5 us
    all_gather x1, waiting for transfers between devices, shards(): lax.all_gather(solve_panel(own_rows, factor), 'loop', axis=0, tiled=True)  29.7 us
  transfers between devices with their start and end apart: 3, of which 3 were waited for; matrix products, arithmetic and copies ran while one was open for 0% of the time, Pallas kernels for 0%

commit v1 on v0

v1 whole, which is shorter than its diff:
```python
import functools
import math

import jax
import jax.numpy as jnp
from jax import lax
from jax.experimental import pallas as pl
from jax.experimental.pallas import tpu as pltpu
from jax.sharding import PartitionSpec as P

F32, BF16 = jnp.float32, jnp.bfloat16
HI = lax.Precision.HIGHEST
MESH = pl.DeviceIdType.MESH
SUB, WIDE, LANES = 8, 128, 128
NT = (((1,), (1,)), ((), ()))
NN = (((1,), (0,)), ((), ()))
DIMS = (4, 8, 2)
SHARES = (((0, 1, 2), 3), ((2, 0, 1), 3), ((1, 0, 2), 2))


def lane_bcast(x, lane):
    return jnp.broadcast_to(x[:, lane:lane + 1], (SUB, WIDE))

def sub_bcast(x, row):
    return jnp.broadcast_to(x[row:row + 1, :], (SUB, WIDE))

def factor_tile(rows):
    lane = lax.broadcasted_iota(jnp.int32, (SUB, WIDE), 1)
    sub = lax.broadcasted_iota(jnp.int32, (SUB, WIDE), 0)
    rows = list(rows)
    count = len(rows)
    scales = []
    for k in range(count):
        base = SUB * k
        here = (lane >= base) & (lane < base + SUB)
        own = rows[k]
        cols = [lane_bcast(own, base + p) for p in range(SUB)]
        own = jnp.where(here, jnp.where(lane - base == sub, 1.0, 0.0), own)
        invs, tops, edges = [], [], {}
        scale = jnp.ones((SUB, WIDE), F32)
        for p in range(SUB):
            inv = 1.0 / sub_bcast(cols[p], p)
            invs.append(inv)
            scale = jnp.where(sub == p, inv, scale)
            top = sub_bcast(own, p)
            tops.append(top)
            if p < SUB - 1:
                mult = jnp.where(sub > p, cols[p] * inv, 0.0)
                for q in range(p + 1, SUB):
                    edges[p, q] = sub_bcast(cols[q], p)
                    cols[q] = cols[q] - mult * edges[p, q]
                own = own - mult * top
        rows[k] = own
        scales.append(scale)
        for i in range(k + 1, count):
            below = [lane_bcast(rows[i], base + p) for p in range(SUB)]
            new = jnp.where(here, 0.0, rows[i])
            for p in range(SUB):
                mult = below[p] * invs[p]
                for q in range(p + 1, SUB):
                    below[q] = below[q] - mult * edges[p, q]
                new = new - mult * tops[p]
            rows[i] = new
    return rows, scales

def factor_inverse(a, w, n):
    tiles = n // WIDE
    lane = lax.broadcasted_iota(jnp.int32, (WIDE, WIDE), 1)
    sub = lax.broadcasted_iota(jnp.int32, (WIDE, WIDE), 0)
    w[...] = jnp.zeros_like(w)
    for j in range(tiles):
        lo, hi = j * WIDE, (j + 1) * WIDE
        rows = [a[lo + SUB * k: lo + SUB * (k + 1), lo:hi] for k in range(WIDE // SUB)]
        rows, scales = factor_tile(rows)
        linv = jnp.concatenate(rows, axis=0)
        linv = jnp.where(lane <= sub, linv, 0.0)
        inv = jnp.concatenate(scales, axis=0)
        root = jnp.sqrt(inv)
        w[lo:hi, lo:hi] = linv * root
        if j + 1 < tiles:
            right = jnp.dot(linv, a[lo:hi, hi:], precision=HI, preferred_element_type=F32)
            mult = lax.dot_general(a[hi:, lo:hi], linv, (((1,), (1,)), ((), ())), precision=HI, preferred_element_type=F32)
        if j:
            left = jnp.dot(linv, a[lo:hi, :lo], precision=HI, preferred_element_type=F32)
            w[lo:hi, :lo] = left * jnp.concatenate([root] * j, axis=1)
        if j + 1 < tiles:
            sc = jnp.concatenate([inv] * (tiles - 1 - j), axis=1)
            a[hi:, hi:] = a[hi:, hi:] - jnp.dot(mult, right * sc, precision=HI, preferred_element_type=F32)
            a[hi:, lo:hi] = -jnp.dot(mult, linv * inv, precision=HI, preferred_element_type=F32)
            if j:
                a[hi:, :lo] = a[hi:, :lo] - jnp.dot(mult, left * jnp.concatenate([inv] * j, axis=1), precision=HI, preferred_element_type=F32)


class Net:
    def __init__(self, dims, send, recv):
        self.dims = dims
        me = lax.axis_index("wide")
        nx, nz, ny = dims
        self.me = (me // (nz * ny), (me // ny) % nz, me % ny)
        self.send, self.recv, self.used = send, recv, 0

    def peer(self, axis, step):
        c = list(self.me)
        c[axis] = lax.rem(c[axis] + step, self.dims[axis])
        return c[axis], (c[0] * self.dims[1] + c[1]) * self.dims[2] + c[2]

    def copy(self, src, dst, wide):
        i = self.used
        self.used += 1
        c = pltpu.make_async_remote_copy(src_ref=src, dst_ref=dst, send_sem=self.send.at[i], recv_sem=self.recv.at[i],
                                         device_id={"wide": wide}, device_id_type=MESH)
        c.start()
        return c

def greet(net):
    barrier = pltpu.get_barrier_semaphore()
    total = 0
    for axis in range(3):
        for step in range(1, net.dims[axis]):
            pl.semaphore_signal(barrier, inc=1, device_id={"wide": net.peer(axis, step)[1]}, device_id_type=MESH)
            total += 1
    pl.semaphore_wait(barrier, total)

class Fraction:
    def __init__(self, net, q, out, start, unit, order, bufs):
        self.net, self.q, self.out, self.start, self.order = net, q, out, start, order
        self.sizes = [net.dims[a] for a in order]
        self.coords = [net.me[a] for a in order]
        n1, n2, n3 = self.sizes
        self.blocks = [unit * n2 * n3, unit * n3, unit]
        self.bufs = bufs
        self.pending = []

    def scatter_start(self, level):
        size = self.blocks[level]
        src, base = (self.q, self.start) if level == 0 else (self.bufs[level - 1][1], 0)
        self.pending = []
        for step in range(1, self.sizes[level]):
            at, wide = self.net.peer(self.order[level], step)
            rows = pl.ds(pl.multiple_of(base + at * size, 8), size)
            self.pending.append(self.net.copy(src.at[rows], self.bufs[level][0].at[step - 1], wide))

    def scatter_finish(self, level):
        size = self.blocks[level]
        src, base = (self.q, self.start) if level == 0 else (self.bufs[level - 1][1], 0)
        for c in self.pending:
            c.wait()
        got, total = self.bufs[level]
        acc = src[pl.ds(pl.multiple_of(base + self.coords[level] * size, 8), size), :]
        for step in range(1, self.sizes[level]):
            acc = acc + got[step - 1]
        if level < 2:
            total[...] = acc
        else:
            self.out[pl.ds(self.offset(2), size), :] = acc

    def offset(self, level):
        at = self.start
        for l in range(level + 1):
            at = at + self.coords[l] * self.blocks[l]
        return pl.multiple_of(at, 8)

    def gather_start(self, level):
        rows = pl.ds(self.offset(level), self.blocks[level])
        self.pending = []
        for step in range(1, self.sizes[level]):
            _, wide = self.net.peer(self.order[level], step)
            self.pending.append(self.net.copy(self.out.at[rows], self.out.at[rows], wide))

    def gather_finish(self):
        for c in self.pending:
            c.wait()

class Diag:
    def __init__(self, net, g):
        self.net, self.g, self.pending = net, g, []

    def view(self, axis):
        x, z, y = self.net.me
        return self.g.at[x, z, y] if axis == 2 else self.g.at[x, z] if axis == 1 else self.g.at[x]

    def start(self, axis):
        self.pending = []
        for step in range(1, self.net.dims[axis]):
            _, wide = self.net.peer(axis, step)
            self.pending.append(self.net.copy(self.view(axis), self.view(axis), wide))

    def finish(self):
        for c in self.pending:
            c.wait()

def plan(dims, total, shares):
    devices = math.prod(dims)
    units = total // (8 * devices)
    out, start = [], 0
    for order, share in shares:
        unit = 8 * share
        out.append((start, unit, order))
        start += unit * devices
    assert start == total
    return out

def scratch_for(dims, parts):
    shapes = []
    for start, unit, order in parts:
        n1, n2, n3 = [dims[a] for a in order]
        shapes += [pltpu.VMEM((n1 - 1, unit * n2 * n3, LANES), F32), pltpu.VMEM((unit * n2 * n3, LANES), F32)]
        shapes += [pltpu.VMEM((n2 - 1, unit * n3, LANES), F32), pltpu.VMEM((unit * n3, LANES), F32)]
        shapes += [pltpu.VMEM((n3 - 1, unit, LANES), F32)]
    return shapes

def pick_kernel(mine, tiles, panel, q):
    t = tiles[pl.program_id(0)] - lax.axis_index("wide") * mine
    held = (t >= 0) & (t < mine)
    for cb in range(q.shape[0]):
        q[cb] = jnp.where(held, panel[:, cb * LANES:(cb + 1) * LANES], 0.0)


def pick_call(panel, tiles, tile):
    m, n = panel.shape
    mine, count = m // tile, tiles.shape[0]

    def place(i, t):
        return jnp.clip(t[i] - lax.axis_index("wide") * mine, 0, mine - 1), 0

    return pl.pallas_call(
        functools.partial(pick_kernel, mine),
        out_shape=jax.ShapeDtypeStruct((n // LANES, count * tile, LANES), F32),
        grid_spec=pltpu.PrefetchScalarGridSpec(
            num_scalar_prefetch=1, grid=(count,),
            in_specs=[pl.BlockSpec((tile, n), place)],
            out_specs=pl.BlockSpec((n // LANES, tile, LANES), lambda i, t: (0, i, 0)),
        ),
    )(tiles, panel)


def gather_kernel(dims, parts, d_ref, q, g_out, q_out, g, out, send, recv, *bufs):
    net = Net(dims, send, recv)
    x, z, y = net.me
    g[x, z, y] = d_ref[...]
    greet(net)
    diag = Diag(net, g)
    diag.start(2)
    fractions = []
    for i, (start, unit, order) in enumerate(parts):
        b = bufs[5 * i:5 * i + 5]
        fractions.append(Fraction(net, q, out, start, unit, order, [(b[0], b[1]), (b[2], b[3]), (b[4], None)]))
    diag.finish()
    diag.start(1)
    diag.finish()
    diag.start(0)
    diag.finish()
    g_out[...] = g[...].reshape(g_out.shape)
    for f in fractions:
        f.scatter_start(0)
    for level in range(3):
        for f in fractions:
            f.scatter_finish(level)
            if level < 2:
                f.scatter_start(level + 1)
            else:
                f.gather_start(2)
    for level in (1, 0):
        for f in fractions:
            f.gather_finish()
            f.gather_start(level)
    for f in fractions:
        f.gather_finish()
    q_out[...] = out[...]

def gather_call(dims, shares, diag, q):
    n, total = diag.shape[1], q.shape[0]
    parts = plan(dims, total, shares)
    count = sum(d - 1 for d in dims)
    sems = count * (1 + 2 * len(parts))
    V = pl.BlockSpec(memory_space=pltpu.VMEM)
    return pl.pallas_call(
        functools.partial(gather_kernel, dims, parts),
        out_shape=(jax.ShapeDtypeStruct((n, n), F32), jax.ShapeDtypeStruct((total, LANES), F32)),
        in_specs=[V, V],
        out_specs=(V, V),
        scratch_shapes=[pltpu.VMEM(dims + (diag.shape[0], n), F32), pltpu.VMEM((total, LANES), F32),
                        pltpu.SemaphoreType.DMA((sems,)), pltpu.SemaphoreType.DMA((sems,))] + scratch_for(dims, parts),
        compiler_params=pltpu.CompilerParams(collective_id=0, has_side_effects=True, vmem_limit_bytes=48 << 20),
    )(diag, q)


def split(x):
    hi = x.astype(BF16)
    return hi, (x - hi.astype(F32)).astype(BF16)

def dot3(a, b, dims):
    def one(x, y):
        return lax.dot_general(x, y, dims, preferred_element_type=F32)
    return one(a[0], b[0]) + (one(a[0], b[1]) + one(a[1], b[0]))

def middle_kernel(d_ref, q_ref, nh_ref, nl_ref, a, w):
    n = d_ref.shape[0]
    a[...] = d_ref[...]
    factor_inverse(a, w, n)
    ws = split(w[...])
    cols = q_ref.shape[0] // (n // LANES)
    step = min(cols, 512)
    for r in range(0, cols, step):
        picked = jnp.concatenate([q_ref[cb * cols + r:cb * cols + r + step, :] for cb in range(n // LANES)], axis=1)
        solved = dot3(split(picked), ws, NT)
        hi, lo = split(dot3(split(solved), ws, NN))
        nh_ref[r:r + step, :] = hi
        nl_ref[r:r + step, :] = lo

def middle_call(d, q):
    n = d.shape[0]
    cols = q.shape[0] // (n // LANES)
    V = pl.BlockSpec(memory_space=pltpu.VMEM)
    return pl.pallas_call(middle_kernel, out_shape=(jax.ShapeDtypeStruct((cols, n), BF16),) * 2,
        in_specs=[V, V], out_specs=(V, V), scratch_shapes=[pltpu.VMEM((n, n), F32)] * 2,
        compiler_params=pltpu.CompilerParams(vmem_limit_bytes=48 << 20))(d, q)

def update_kernel(tile, mask, p_ref, t_ref, nh_ref, nl_ref, o_ref):
    per = p_ref.shape[0] // tile
    first = pl.program_id(0) * per
    u = dot3(split(p_ref[...]), (nh_ref[...], nl_ref[...]), NT)
    for i in range(per):
        for j in range(t_ref.shape[1] // tile):
            r, c = slice(i * tile, (i + 1) * tile), slice(j * tile, (j + 1) * tile)
            t = t_ref[r, c]
            o_ref[r, c] = t - jnp.where(mask[first + i, j] != 0, u[r, c], 0.0)

def update_call(panel, trailing, mask, nh, nl, tile, rows=512):
    m, n = panel.shape
    cols = trailing.shape[1]
    whole = pl.BlockSpec((cols, n), lambda i: (0, 0))
    block = pl.BlockSpec((rows, cols), lambda i: (i, 0))
    return pl.pallas_call(functools.partial(update_kernel, tile),
        out_shape=jax.ShapeDtypeStruct(trailing.shape, F32), grid=(m // rows,),
        in_specs=[pl.BlockSpec(memory_space=pltpu.SMEM), pl.BlockSpec((rows, n), lambda i: (i, 0)), block, whole, whole],
        out_specs=block,
        compiler_params=pltpu.CompilerParams(vmem_limit_bytes=56 << 20))(mask, panel, trailing, nh, nl)


def shards(diag_block, panel, trailing, fill_mask, column_tiles):
    tile = trailing.shape[1] // column_tiles.shape[0]
    local = pick_call(panel, column_tiles, tile).reshape(-1, LANES)
    diag, picked = gather_call(DIMS, SHARES, diag_block, local)
    high, low = middle_call(diag, picked)
    return update_call(panel, trailing, fill_mask, high, low, tile)


def solution(mesh):
    return jax.shard_map(
        shards,
        mesh=mesh,
        in_specs=(P("wide", None), P("wide", None), P("wide", "loop"), P("wide", "loop"), P("loop")),
        out_specs=P("wide", "loop"),
        check_vma=False,
    )
```

time: 1180 us -> 125 us (0.11)
  waiting for transfers between devices: 939 us -> 0 us
  other arithmetic: 143 us -> 0 us
  Pallas kernels: 0 us -> 120 us
  local copies, waits for them, and re-layouts: 37.7 us -> 4.95 us
  matrix products: 32 us -> 0 us
  between operations: 16.2 us -> 0.03 us
    psum x1 -> x0, waiting for transfers between devices: 612 us -> none  [shards(): lax.psum(local_pick, 'wide').reshape(col_tiles * tile_size, panel_width)]
    all_gather x2 -> x0, waiting for transfers between devices: 327 us -> none  [the longest x1 297 us: shards(): gathered = lax.all_gather(diag_block, 'wide', axis=0, tiled=True)]
    another operation x17 -> x0, other arithmetic: 135 us -> none  [the longest x14 92.9 us: shards(): factor = jnp.linalg.cholesky(gathered)]
    pallas_call x0 -> x4, Pallas kernels: none -> 120 us  [the longest x1 82 us: gather_call(): pl.pallas_call(functools.partial(gather_kernel, dims, parts), out_shape=(...]
    dot_general x2 -> x0, matrix products: 17.6 us -> none  [the longest x1 13.9 us: shards(): lax.dot_general(lower_panel, picked, (((1,), (1,)), ((), ())), precision=...]
    another operation x17 -> x0, local copies, waits for them, and re-layouts: 15.2 us -> none
    another operation x13 -> x0, matrix products: 14.4 us -> none  [the longest x6 7.76 us: shards(): factor = jnp.linalg.cholesky(gathered)]
  transfers between devices with their start and end apart: 3 -> 0, of which waited for: 3 -> 0; matrix products, arithmetic and copies ran while one was open for 0% -> 0% of each run, Pallas kernels for 0% -> 0%
where the time goes in v1:
time: 125 us
  Pallas kernels  120 us (96%)
  local copies, waits for them, and re-layouts  4.95 us (4%)
    pallas_call x1, Pallas kernels, gather_call(): pl.pallas_call(functools.partial(gather_kernel, dims, parts), out_shape=(...  82 us
    pallas_call x1, Pallas kernels, middle_call(): pl.pallas_call(middle_kernel, out_shape=(jax.ShapeDtypeStruct((cols, n),...  22.8 us
    pallas_call x1, Pallas kernels, update_call(): pl.pallas_call(functools.partial(update_kernel, tile), out_shape=jax.Shap...  10.2 us
    unnamed x9, local copies, waits for them, and re-layouts  4.95 us
    pallas_call x1, Pallas kernels, pick_call(): pl.pallas_call(functools.partial(pick_kernel, mine), out_shape=jax.ShapeD...  4.69 us

profile of v1, /device:TPU:16, one launch (start us, length us, event | category | flops | bytes accessed | tf_op | source)
XLA Modules:
  0.0 124.6 jit_solution(4969480564830758350)
XLA Ops:
  0.0 0.0 copy-start.3
  0.0 1.4 %copy.6.mask = s32[12,8]{1,0:T(8,128)} copy(s32[12,8]{0,1:T(8,128)} %param.8) | data formatting | bytes 768 | tf_op args[3]
  1.4 4.7 %shard_map.55 = f32[4,1024,128]{2,1,0:T(8,128)} custom-call(s32[8]{0:T(128)} %tiles.1, f32[1536,512]{1,0:T(8,128)} %p_ref.1), custom_call_target="tpu_custom_call" | custom-call | tf_op jit(solution)/shard_map/pallas_call | solution.py:226
  6.1 0.0 copy-done.3
  6.1 0.0 copy-start
  6.1 1.6 %copy-done = f32[4,1024,128]{2,1,0:T(8,128)S(1)} copy-done((f32[4,1024,128]{2,1,0:T(8,128)S(1)}, f32[4,1024,128]{2,1,0:T(8,128)}, u32[]{:S(2)}) %copy-start) | copy-done | bytes 2097176
  7.7 82.0 %shard_map.56 = (f32[512,512]{1,0:T(8,128)S(1)}, f32[4096,128]{1,0:T(8,128)S(1)}) custom-call(f32[8,512]{1,0:T(8,128)S(1)} %copy-done.3, f32[4096,128]{1,0:T(8,128)S(1)} %bitcast.1), custom_call_target="tpu_custom_call" | custom-call | tf_op jit(solution)/shard_map/pallas_call | solution.py:277
  89.6 22.8 %shard_map.57 = (bf16[1024,512]{1,0:T(8,128)(2,1)S(1)}, bf16[1024,512]{1,0:T(8,128)(2,1)S(1)}) custom-call(f32[512,512]{1,0:T(8,128)S(1)} %get-tuple-element.9.d_ref, f32[4096,128]{1,0:T(8,128)S(1)} %get-tuple-element.10.q_ref), custom_call_target="tpu_custom_call" | custom-call | tf_op jit(solution)/shard_map/pallas_call | solution.py:315
  112.4 0.0 copy-start.1
  112.5 1.0 copy-done.1
  113.4 0.0 copy-start.2
  113.4 1.0 copy-done.2
  114.4 10.2 %shard_map.58 = f32[1536,1024]{1,0:T(8,128)} custom-call(s32[12,8]{1,0:T(8,128)} %copy.6.mask, f32[1536,512]{1,0:T(8,128)} %p_ref.1, f32[1536,1024]{1,0:T(8,128)} %t_ref.1, bf16[1024,512]{1,0:T(8,128)(2,1)} %copy-done.1, bf16[1024,512]{1,0:T(8,128)(2,1)} %copy-done.2), custom_call_target="tpu_custom_call" | custom-call | tf_op jit(solution)/shard_map/pallas_call | solution.py:334
Async XLA Ops:
  0.0 6.1 %copy-start.3 = (f32[8,512]{1,0:T(8,128)S(1)}, f32[8,512]{1,0:T(8,128)}, u32[]{:S(2)}) copy-start(f32[8,512]{1,0:T(8,128)} %d_ref.1) | copy-start | bytes 49156
  6.1 1.6 %copy-start = (f32[4,1024,128]{2,1,0:T(8,128)S(1)}, f32[4,1024,128]{2,1,0:T(8,128)}, u32[]{:S(2)}) copy-start(f32[4,1024,128]{2,1,0:T(8,128)} %shard_map.55) | copy-start | bytes 6291460
  112.4 1.0 copy-start.1
  113.4 1.0 copy-start.2

commit v2 on v1

--- a/solution.py
+++ b/solution.py
@@ -15,6 +15,7 @@
 NT = (((1,), (1,)), ((), ()))
 NN = (((1,), (0,)), ((), ()))
 DIMS = (4, 8, 2)
+HOOKS = {20: 6, 32: 6, 40: 6, 46: 6, 54: 6}
 SHARES = (((0, 1, 2), 3), ((2, 0, 1), 3), ((1, 0, 2), 2))
 
 
@@ -24,7 +25,7 @@
 def sub_bcast(x, row):
     return jnp.broadcast_to(x[row:row + 1, :], (SUB, WIDE))
 
-def factor_tile(rows):
+def factor_tile(rows, hook):
     lane = lax.broadcasted_iota(jnp.int32, (SUB, WIDE), 1)
     sub = lax.broadcasted_iota(jnp.int32, (SUB, WIDE), 0)
     rows = list(rows)
@@ -61,34 +62,37 @@
                     below[q] = below[q] - mult * edges[p, q]
                 new = new - mult * tops[p]
             rows[i] = new
+        hook()
     return rows, scales
 
-def factor_inverse(a, w, n):
+def factor_inverse(block, a, w, hook):
+    n = a.shape[0]
     tiles = n // WIDE
     lane = lax.broadcasted_iota(jnp.int32, (WIDE, WIDE), 1)
     sub = lax.broadcasted_iota(jnp.int32, (WIDE, WIDE), 0)
     w[...] = jnp.zeros_like(w)
     for j in range(tiles):
         lo, hi = j * WIDE, (j + 1) * WIDE
+        block(j)
         rows = [a[lo + SUB * k: lo + SUB * (k + 1), lo:hi] for k in range(WIDE // SUB)]
-        rows, scales = factor_tile(rows)
-        linv = jnp.concatenate(rows, axis=0)
-        linv = jnp.where(lane <= sub, linv, 0.0)
+        rows, scales = factor_tile(rows, lambda: hook(j))
+        linv = jnp.where(lane <= sub, jnp.concatenate(rows, axis=0), 0.0)
         inv = jnp.concatenate(scales, axis=0)
         root = jnp.sqrt(inv)
         w[lo:hi, lo:hi] = linv * root
         if j + 1 < tiles:
             right = jnp.dot(linv, a[lo:hi, hi:], precision=HI, preferred_element_type=F32)
-            mult = lax.dot_general(a[hi:, lo:hi], linv, (((1,), (1,)), ((), ())), precision=HI, preferred_element_type=F32)
+            mult = lax.dot_general(a[hi:, lo:hi], linv, NT, precision=HI, preferred_element_type=F32)
         if j:
             left = jnp.dot(linv, a[lo:hi, :lo], precision=HI, preferred_element_type=F32)
             w[lo:hi, :lo] = left * jnp.concatenate([root] * j, axis=1)
         if j + 1 < tiles:
-            sc = jnp.concatenate([inv] * (tiles - 1 - j), axis=1)
-            a[hi:, hi:] = a[hi:, hi:] - jnp.dot(mult, right * sc, precision=HI, preferred_element_type=F32)
+            scaled = right * jnp.concatenate([inv] * (tiles - 1 - j), axis=1)
+            a[hi:, hi:] = a[hi:, hi:] - jnp.dot(mult, scaled, precision=HI, preferred_element_type=F32)
             a[hi:, lo:hi] = -jnp.dot(mult, linv * inv, precision=HI, preferred_element_type=F32)
             if j:
-                a[hi:, :lo] = a[hi:, :lo] - jnp.dot(mult, left * jnp.concatenate([inv] * j, axis=1), precision=HI, preferred_element_type=F32)
+                scaled = left * jnp.concatenate([inv] * j, axis=1)
+                a[hi:, :lo] = a[hi:, :lo] - jnp.dot(mult, scaled, precision=HI, preferred_element_type=F32)
 
 
 class Net:
@@ -209,112 +213,113 @@
         shapes += [pltpu.VMEM((n3 - 1, unit, LANES), F32)]
     return shapes
 
-def pick_kernel(mine, tiles, panel, q):
-    t = tiles[pl.program_id(0)] - lax.axis_index("wide") * mine
-    held = (t >= 0) & (t < mine)
-    for cb in range(q.shape[0]):
-        q[cb] = jnp.where(held, panel[:, cb * LANES:(cb + 1) * LANES], 0.0)
-
-
-def pick_call(panel, tiles, tile):
-    m, n = panel.shape
-    mine, count = m // tile, tiles.shape[0]
-
-    def place(i, t):
-        return jnp.clip(t[i] - lax.axis_index("wide") * mine, 0, mine - 1), 0
-
-    return pl.pallas_call(
-        functools.partial(pick_kernel, mine),
-        out_shape=jax.ShapeDtypeStruct((n // LANES, count * tile, LANES), F32),
-        grid_spec=pltpu.PrefetchScalarGridSpec(
-            num_scalar_prefetch=1, grid=(count,),
-            in_specs=[pl.BlockSpec((tile, n), place)],
-            out_specs=pl.BlockSpec((n // LANES, tile, LANES), lambda i, t: (0, i, 0)),
-        ),
-    )(tiles, panel)
-
-
-def gather_kernel(dims, parts, d_ref, q, g_out, q_out, g, out, send, recv, *bufs):
+def split(x):
+    hi = x.astype(BF16)
+    return hi, (x - hi.astype(F32)).astype(BF16)
+
+def dot3(a, b, dims):
+    def one(x, y):
+        return lax.dot_general(x, y, dims, preferred_element_type=F32)
+    return one(a[0], b[0]) + (one(a[0], b[1]) + one(a[1], b[0]))
+
+def select_rows(panel, tiles, q, tile):
+    mine = panel.shape[0] // tile
+    count = tiles.shape[0]
+    first = lax.axis_index("wide") * mine
+    wanted = [jnp.full((SUB, LANES), tiles[c] - first, jnp.int32) for c in range(count)]
+
+    def step(r, carry):
+        for cb in range(panel.shape[1] // LANES):
+            picked = [jnp.zeros((SUB, LANES), F32)] * count
+            for i in range(mine):
+                block = panel[pl.ds(pl.multiple_of(i * tile + r * SUB, SUB), SUB), cb * LANES:(cb + 1) * LANES]
+                picked = [jnp.where(w == i, block, p) for w, p in zip(wanted, picked)]
+            for c in range(count):
+                q[pl.ds(pl.multiple_of((cb * count + c) * tile + r * SUB, SUB), SUB), :] = picked[c]
+        return carry
+
+    lax.fori_loop(0, tile // SUB, step, 0)
+
+
+def front_kernel(dims, parts, tile, d_ref, panel_hbm, tiles, nh_ref, nl_ref, panel, q, g, a, w, out, local, send, recv, *bufs):
     net = Net(dims, send, recv)
     x, z, y = net.me
+    load = pltpu.make_async_copy(panel_hbm, panel, local)
+    load.start()
     g[x, z, y] = d_ref[...]
     greet(net)
     diag = Diag(net, g)
     diag.start(2)
+    load.wait()
+    select_rows(panel, tiles, q, tile)
+    diag.finish()
+    diag.start(1)
     fractions = []
     for i, (start, unit, order) in enumerate(parts):
         b = bufs[5 * i:5 * i + 5]
         fractions.append(Fraction(net, q, out, start, unit, order, [(b[0], b[1]), (b[2], b[3]), (b[4], None)]))
     diag.finish()
-    diag.start(1)
-    diag.finish()
     diag.start(0)
-    diag.finish()
-    g_out[...] = g[...].reshape(g_out.shape)
     for f in fractions:
         f.scatter_start(0)
+
+    steps = []
     for level in range(3):
         for f in fractions:
-            f.scatter_finish(level)
-            if level < 2:
-                f.scatter_start(level + 1)
-            else:
-                f.gather_start(2)
+            steps.append(functools.partial(f.scatter_finish, level))
+            steps.append(functools.partial(f.scatter_start, level + 1) if level < 2 else functools.partial(f.gather_start, 2))
     for level in (1, 0):
         for f in fractions:
-            f.gather_finish()
-            f.gather_start(level)
+            steps.append(f.gather_finish)
+            steps.append(functools.partial(f.gather_start, level))
     for f in fractions:
-        f.gather_finish()
-    q_out[...] = out[...]
-
-def gather_call(dims, shares, diag, q):
-    n, total = diag.shape[1], q.shape[0]
-    parts = plan(dims, total, shares)
-    count = sum(d - 1 for d in dims)
-    sems = count * (1 + 2 * len(parts))
-    V = pl.BlockSpec(memory_space=pltpu.VMEM)
-    return pl.pallas_call(
-        functools.partial(gather_kernel, dims, parts),
-        out_shape=(jax.ShapeDtypeStruct((n, n), F32), jax.ShapeDtypeStruct((total, LANES), F32)),
-        in_specs=[V, V],
-        out_specs=(V, V),
-        scratch_shapes=[pltpu.VMEM(dims + (diag.shape[0], n), F32), pltpu.VMEM((total, LANES), F32),
-                        pltpu.SemaphoreType.DMA((sems,)), pltpu.SemaphoreType.DMA((sems,))] + scratch_for(dims, parts),
-        compiler_params=pltpu.CompilerParams(collective_id=0, has_side_effects=True, vmem_limit_bytes=48 << 20),
-    )(diag, q)
-
-
-def split(x):
-    hi = x.astype(BF16)
-    return hi, (x - hi.astype(F32)).astype(BF16)
-
-def dot3(a, b, dims):
-    def one(x, y):
-        return lax.dot_general(x, y, dims, preferred_element_type=F32)
-    return one(a[0], b[0]) + (one(a[0], b[1]) + one(a[1], b[0]))
-
-def middle_kernel(d_ref, q_ref, nh_ref, nl_ref, a, w):
-    n = d_ref.shape[0]
-    a[...] = d_ref[...]
-    factor_inverse(a, w, n)
+        steps.append(f.gather_finish)
+    calls = [0]
+
+    def hook(j):
+        at = HOOKS.get(calls[0])
+        calls[0] += 1
+        for _ in range(at or 0):
+            steps.pop(0)()
+
+    n = a.shape[0]
+
+    def block(j):
+        if j == 0:
+            diag.finish()
+            a[...] = g[...].reshape(n, n)
+
+    factor_inverse(block, a, w, hook)
+    while steps:
+        steps.pop(0)()
     ws = split(w[...])
-    cols = q_ref.shape[0] // (n // LANES)
+    cols = out.shape[0] // (n // LANES)
     step = min(cols, 512)
     for r in range(0, cols, step):
-        picked = jnp.concatenate([q_ref[cb * cols + r:cb * cols + r + step, :] for cb in range(n // LANES)], axis=1)
+        picked = jnp.concatenate([out[cb * cols + r:cb * cols + r + step, :] for cb in range(n // LANES)], axis=1)
         solved = dot3(split(picked), ws, NT)
         hi, lo = split(dot3(split(solved), ws, NN))
         nh_ref[r:r + step, :] = hi
         nl_ref[r:r + step, :] = lo
 
-def middle_call(d, q):
-    n = d.shape[0]
-    cols = q.shape[0] // (n // LANES)
+
+def front_call(dims, shares, tile, diag, panel, tiles):
+    n, cols = panel.shape[1], tiles.shape[0] * tile
+    total = cols * (n // LANES)
+    parts = plan(dims, total, shares)
+    sems = sum(d - 1 for d in dims) * (1 + 2 * len(parts))
     V = pl.BlockSpec(memory_space=pltpu.VMEM)
-    return pl.pallas_call(middle_kernel, out_shape=(jax.ShapeDtypeStruct((cols, n), BF16),) * 2,
-        in_specs=[V, V], out_specs=(V, V), scratch_shapes=[pltpu.VMEM((n, n), F32)] * 2,
-        compiler_params=pltpu.CompilerParams(vmem_limit_bytes=48 << 20))(d, q)
+    return pl.pallas_call(
+        functools.partial(front_kernel, dims, parts, tile),
+        out_shape=(jax.ShapeDtypeStruct((cols, n), BF16),) * 2,
+        in_specs=[V, pl.BlockSpec(memory_space=pl.ANY), pl.BlockSpec(memory_space=pltpu.SMEM)],
+        out_specs=(V, V),
+        scratch_shapes=[pltpu.VMEM(panel.shape, F32), pltpu.VMEM((total, LANES), F32), pltpu.VMEM(dims + (diag.shape[0], n), F32),
+                        pltpu.VMEM((n, n), F32), pltpu.VMEM((n, n), F32), pltpu.VMEM((total, LANES), F32), pltpu.SemaphoreType.DMA,
+                        pltpu.SemaphoreType.DMA((sems,)), pltpu.SemaphoreType.DMA((sems,))] + scratch_for(dims, parts),
+        compiler_params=pltpu.CompilerParams(collective_id=0, has_side_effects=True, vmem_limit_bytes=56 << 20),
+    )(diag, panel, tiles)
+
 
 def update_kernel(tile, mask, p_ref, t_ref, nh_ref, nl_ref, o_ref):
     per = p_ref.shape[0] // tile
@@ -340,9 +345,7 @@
 
 def shards(diag_block, panel, trailing, fill_mask, column_tiles):
     tile = trailing.shape[1] // column_tiles.shape[0]
-    local = pick_call(panel, column_tiles, tile).reshape(-1, LANES)
-    diag, picked = gather_call(DIMS, SHARES, diag_block, local)
-    high, low = middle_call(diag, picked)
+    high, low = front_call(DIMS, SHARES, tile, diag_block, panel, column_tiles)
     return update_call(panel, trailing, fill_mask, high, low, tile)
 
 

time: 125 us -> 95.5 us (0.76)
  Pallas kernels: 120 us -> 92.5 us
  local copies, waits for them, and re-layouts: 4.95 us -> 1.35 us
    pallas_call x3 -> x1, Pallas kernels: 109 us -> 82.3 us  [front_call(): pl.pallas_call(functools.partial(front_kernel, dims, parts, tile), out_sh...]
    unnamed x9 -> x1, local copies, waits for them, and re-layouts: 4.95 us -> 1.35 us
where the time goes in v2:
time: 95.5 us; the launch traced here: 93.9 us
  Pallas kernels  92.5 us (97%)
  local copies, waits for them, and re-layouts  1.35 us (1%)
    pallas_call x1, Pallas kernels, front_call(): pl.pallas_call(functools.partial(front_kernel, dims, parts, tile), out_sh...  82.3 us
    pallas_call x1, Pallas kernels, update_call(): pl.pallas_call(functools.partial(update_kernel, tile), out_shape=jax.Shap...  10.2 us

profile of v2, /device:TPU:16, one launch (start us, length us, event | category | flops | bytes accessed | tf_op | source)
XLA Modules:
  0.0 93.9 jit_solution(12700866771025639048)
XLA Ops:
  0.0 1.4 %copy.6.mask = s32[12,8]{1,0:T(8,128)} copy(s32[12,8]{0,1:T(8,128)} %param.8) | data formatting | bytes 768 | tf_op args[3]
  1.4 82.3 %shard_map.55 = (bf16[1024,512]{1,0:T(8,128)(2,1)}, bf16[1024,512]{1,0:T(8,128)(2,1)}) custom-call(f32[8,512]{1,0:T(8,128)} %d_ref.1, f32[1536,512]{1,0:T(8,128)} %p_ref.1, s32[8]{0:T(128)} %tiles.1), custom_call_target="tpu_custom_call" | custom-call | tf_op jit(solution)/shard_map/pallas_call | solution.py:312
  83.7 10.2 %shard_map.56 = f32[1536,1024]{1,0:T(8,128)} custom-call(s32[12,8]{1,0:T(8,128)} %copy.6.mask, f32[1536,512]{1,0:T(8,128)} %p_ref.1, f32[1536,1024]{1,0:T(8,128)} %t_ref.1, bf16[1024,512]{1,0:T(8,128)(2,1)} %get-tuple-element.7.nh_ref, bf16[1024,512]{1,0:T(8,128)(2,1)} %get-tuple-element.8.nl_ref), custom_call_target="tpu_custom_call" | custom-call | tf_op jit(solution)/shard_map/pallas_call | solution.py:339

commit v3 on v2

v3 whole, which is shorter than its diff:
```python
import functools
import math

import jax
import jax.numpy as jnp
from jax import lax
from jax.experimental import pallas as pl
from jax.experimental.pallas import tpu as pltpu
from jax.sharding import PartitionSpec as P

F32, BF16 = jnp.float32, jnp.bfloat16
HI = lax.Precision.HIGHEST
MESH = pl.DeviceIdType.MESH
SUB, WIDE, LANES = 8, 128, 128
NT = (((1,), (1,)), ((), ()))
NN = (((1,), (0,)), ((), ()))
DIMS = (4, 8, 2)
ORDERS = (
    (0, 2, 1),
    (2, 0, 1),
    (2, 0, 1),
    (1, 0, 2),
    (0, 2, 1),
    (1, 0, 2),
    (2, 0, 1),
    (2, 0, 1),
)
BEFORE = (1, 0, -1, 2, 4, 1, 3, 6)
LATER = (
    (0, 7), (0, 2), (0, 0), (0, 3), (0, 4), (3, 6), (3, 5), (5, 1),
    (7, 3), (9, 7), (10, 2), (12, 0), (13, 5), (14, 4), (14, 3), (16, 6),
    (18, 1), (21, 5), (21, 7), (23, 2), (24, 3), (25, 0), (27, 4), (29, 5),
    (29, 6), (30, 1), (34, 7), (35, 0), (36, 2), (37, 4), (38, 5), (42, 6),
    (46, 1), (46, 7), (50, 3), (53, 2), (54, 0), (61, 6), (61, 4), (65, 5),
    (69, 7),
)


def lane_bcast(x, lane):
    return jnp.broadcast_to(x[:, lane:lane + 1], (SUB, WIDE))

def sub_bcast(x, row):
    return jnp.broadcast_to(x[row:row + 1, :], (SUB, WIDE))

def factor_tile(rows, hook):
    lane = lax.broadcasted_iota(jnp.int32, (SUB, WIDE), 1)
    sub = lax.broadcasted_iota(jnp.int32, (SUB, WIDE), 0)
    rows = list(rows)
    count = len(rows)
    scales = []
    for k in range(count):
        base = SUB * k
        here = (lane >= base) & (lane < base + SUB)
        own = rows[k]
        cols = [lane_bcast(own, base + p) for p in range(SUB)]
        own = jnp.where(here, jnp.where(lane - base == sub, 1.0, 0.0), own)
        invs, tops, edges = [], [], {}
        scale = jnp.ones((SUB, WIDE), F32)
        for p in range(SUB):
            inv = 1.0 / sub_bcast(cols[p], p)
            invs.append(inv)
            scale = jnp.where(sub == p, inv, scale)
            top = sub_bcast(own, p)
            tops.append(top)
            if p < SUB - 1:
                mult = jnp.where(sub > p, cols[p] * inv, 0.0)
                for q in range(p + 1, SUB):
                    edges[p, q] = sub_bcast(cols[q], p)
                    cols[q] = cols[q] - mult * edges[p, q]
                own = own - mult * top
        rows[k] = own
        scales.append(scale)
        for i in range(k + 1, count):
            below = [lane_bcast(rows[i], base + p) for p in range(SUB)]
            new = jnp.where(here, 0.0, rows[i])
            for p in range(SUB):
                mult = below[p] * invs[p]
                for q in range(p + 1, SUB):
                    below[q] = below[q] - mult * edges[p, q]
                new = new - mult * tops[p]
            rows[i] = new
        hook()
    return rows, scales

def factor_inverse(a, w, hook):
    n = a.shape[0]
    tiles = n // WIDE
    lane = lax.broadcasted_iota(jnp.int32, (WIDE, WIDE), 1)
    sub = lax.broadcasted_iota(jnp.int32, (WIDE, WIDE), 0)
    w[...] = jnp.zeros_like(w)
    for j in range(tiles):
        lo, hi = j * WIDE, (j + 1) * WIDE
        rows = [a[lo + SUB * k: lo + SUB * (k + 1), lo:hi] for k in range(WIDE // SUB)]
        rows, scales = factor_tile(rows, hook)
        linv = jnp.where(lane <= sub, jnp.concatenate(rows, axis=0), 0.0)
        inv = jnp.concatenate(scales, axis=0)
        root = jnp.sqrt(inv)
        w[lo:hi, lo:hi] = linv * root
        if j + 1 < tiles:
            right = jnp.dot(linv, a[lo:hi, hi:], precision=HI, preferred_element_type=F32)
            mult = lax.dot_general(a[hi:, lo:hi], linv, NT, precision=HI, preferred_element_type=F32)
        if j:
            left = jnp.dot(linv, a[lo:hi, :lo], precision=HI, preferred_element_type=F32)
            w[lo:hi, :lo] = left * jnp.concatenate([root] * j, axis=1)
        if j + 1 < tiles:
            scaled = right * jnp.concatenate([inv] * (tiles - 1 - j), axis=1)
            a[hi:, hi:] = a[hi:, hi:] - jnp.dot(mult, scaled, precision=HI, preferred_element_type=F32)
            a[hi:, lo:hi] = -jnp.dot(mult, linv * inv, precision=HI, preferred_element_type=F32)
            if j:
                scaled = left * jnp.concatenate([inv] * j, axis=1)
                a[hi:, :lo] = a[hi:, :lo] - jnp.dot(mult, scaled, precision=HI, preferred_element_type=F32)


class Net:
    def __init__(self, dims, send, recv):
        self.dims = dims
        me = lax.axis_index("wide")
        nx, nz, ny = dims
        self.me = (me // (nz * ny), (me // ny) % nz, me % ny)
        loop = lax.axis_index("loop")
        self.core = lax.rem(loop, 2)
        self.twin = {"loop": loop + 1 - 2 * self.core}
        self.send, self.recv, self.used, self.sent = send, recv, 0, []

    def peer(self, steps):
        c = [lax.rem(c + s, n) for c, s, n in zip(self.me, steps, self.dims)]
        return c, {"wide": (c[0] * self.dims[1] + c[1]) * self.dims[2] + c[2]}

    def along(self, axis, step):
        c, device = self.peer([step if a == axis else 0 for a in range(3)])
        return c[axis], device

    def plane(self):
        steps = [(0, dz, dy) for dz in range(self.dims[1]) for dy in range(self.dims[2]) if dz or dy]
        return sorted(steps, key=lambda s: -min(s[1], self.dims[1] - s[1]) - s[2])

    def slot(self):
        self.used += 1
        return self.used - 1

    def copy(self, src, dst, device, slot):
        pltpu.make_async_remote_copy(
            src_ref=src, dst_ref=dst, send_sem=self.send.at[slot], recv_sem=self.recv.at[slot], device_id=device, device_id_type=MESH
        ).start()

    def arrived(self, like, slot):
        pltpu.make_async_copy(like, like, self.recv.at[slot]).wait()
        self.sent.append((like, slot))

    def drain(self):
        for like, slot in self.sent:
            pltpu.make_async_copy(like, like, self.send.at[slot]).wait()

    def greet(self):
        devices = [self.peer(s)[1] for s in self.plane()] + [self.along(0, s)[1] for s in range(1, self.dims[0])] + [self.twin]
        for device in devices:
            pl.semaphore_signal(pltpu.get_barrier_semaphore(), inc=1, device_id=device, device_id_type=MESH)
        return len(devices)


class Reduced:
    def __init__(self, net, q, out, start, unit, order, bufs):
        self.net, self.q, self.out, self.start, self.order = net, q, out, start, order
        self.sizes = [net.dims[a] for a in order]
        self.coords = [net.me[a] for a in order]
        n1, n2, n3 = self.sizes
        self.blocks = [unit * n2 * n3, unit * n3, unit]
        self.bufs = bufs
        self.stage = 0

    def offset(self, level):
        at = self.start
        for l in range(level + 1):
            at = at + self.coords[l] * self.blocks[l]
        return pl.multiple_of(at, SUB)

    def source(self, level):
        return (self.q, self.start) if level == 0 else (self.bufs[level - 1][1], 0)

    def begin(self):
        self.slot = self.net.slot()
        level = min(self.stage, 5 - self.stage)
        size = self.blocks[level]
        for step in range(1, self.sizes[level]):
            at, device = self.net.along(self.order[level], step)
            if self.stage < 3:
                src, base = self.source(level)
                rows = pl.ds(pl.multiple_of(base + at * size, SUB), size)
                self.net.copy(src.at[rows], self.bufs[level][0].at[pl.ds((step - 1) * size, size)], device, self.slot)
            else:
                rows = pl.ds(self.offset(level), size)
                self.net.copy(self.out.at[rows], self.out.at[rows], device, self.slot)

    def finish(self):
        level = min(self.stage, 5 - self.stage)
        size, others = self.blocks[level], self.sizes[level] - 1
        if self.stage < 3:
            got, total = self.bufs[level]
            self.net.arrived(got, self.slot)
            src, base = self.source(level)
            acc = src[pl.ds(pl.multiple_of(base + self.coords[level] * size, SUB), size), :]
            for step in range(others):
                acc = acc + got[step * size:(step + 1) * size, :]
            if level < 2:
                total[...] = acc
            else:
                self.out[pl.ds(self.offset(2), size), :] = acc
        else:
            self.net.arrived(self.out.at[pl.ds(self.start, others * size)], self.slot)
        self.stage += 1

    def advance(self):
        self.finish()
        if self.stage < 6:
            self.begin()


class Diag:
    def __init__(self, net, g, like):
        self.net, self.g, self.like = net, g, like

    def spread(self):
        x, z, y = self.net.me
        own = self.g.at[self.net.core, x, z, y]
        self.slot = self.net.slot()
        for steps in self.net.plane():
            self.net.copy(own, own, self.net.peer(steps)[1], self.slot)

    def cross(self):
        nx, nz, ny = self.net.dims
        shape = self.g.shape
        self.net.arrived(self.like.at[pl.ds(0, (nz * ny - 1) * shape[4] * shape[5] // LANES)], self.slot)
        own = self.g.at[self.net.core, self.net.me[0]]
        self.slots = [self.net.slot() for _ in range(2 * nx)]
        for step in range(1, nx):
            self.net.copy(own, own, self.net.along(0, step)[1], self.slots[step])
        self.net.copy(own, own, self.net.twin, self.slots[nx])

    def swap(self):
        nx = self.net.dims[0]
        for step in range(1, nx):
            self.net.arrived(self.g.at[0, 0], self.slots[step])
            block = self.g.at[self.net.core, lax.rem(self.net.me[0] + nx - step, nx)]
            self.net.copy(block, block, self.net.twin, self.slots[nx + step])
        for step in range(nx):
            self.net.arrived(self.g.at[0, 0], self.slots[nx + step])


def scratch_for(dims, unit, orders):
    shapes = []
    for order in orders:
        n1, n2, n3 = [dims[a] for a in order]
        for level, (n, size) in enumerate(((n1, unit * n2 * n3), (n2, unit * n3), (n3, unit))):
            shapes += [pltpu.VMEM(((n - 1) * size, LANES), F32)] + [pltpu.VMEM((size, LANES), F32)] * (level < 2)
    return shapes


def split(x):
    hi = x.astype(BF16)
    return hi, (x - hi.astype(F32)).astype(BF16)

def dot3(a, b, dims):
    def one(x, y):
        return lax.dot_general(x, y, dims, preferred_element_type=F32)
    return one(a[0], b[0]) + (one(a[0], b[1]) + one(a[1], b[0]))

def select_rows(panel, tiles, q, tile):
    mine = panel.shape[0] // tile
    count, blocks = tiles.shape[0], panel.shape[1] // LANES
    first = lax.axis_index("wide") * mine
    wanted = [jnp.full((SUB, LANES), tiles[c] - first, jnp.int32) for c in range(count)]

    def step(r, carry):
        for cb in range(blocks):
            picked = [jnp.zeros((SUB, LANES), F32)] * count
            for i in range(mine):
                block = panel[pl.ds(pl.multiple_of(i * tile + r * SUB, SUB), SUB), cb * LANES:(cb + 1) * LANES]
                picked = [jnp.where(w == i, block, p) for w, p in zip(wanted, picked)]
            for c in range(count):
                q[pl.ds(pl.multiple_of((c * blocks + cb) * tile + r * SUB, SUB), SUB), :] = picked[c]
        return carry

    lax.fori_loop(0, tile // SUB, step, 0)


def front_kernel(dims, orders, tile, d_ref, panel_hbm, tiles, nh_ref, nl_ref, panel, q, g, a, w, out, local, send, recv, *bufs):
    n = a.shape[0]
    blocks = n // LANES
    half = n // 2
    net = Net(dims, send, recv)
    load = pltpu.make_async_copy(panel_hbm, panel, local)
    load.start()
    greeted = net.greet()
    g[net.core, net.me[0], net.me[1], net.me[2]] = d_ref[:, pl.ds(pl.multiple_of(net.core * half, LANES), half)]
    load.wait()
    select_rows(panel, tiles, q, tile)
    pl.semaphore_wait(pltpu.get_barrier_semaphore(), greeted)

    diag = Diag(net, g, q)
    diag.spread()
    rows = tile * blocks
    unit = rows // math.prod(dims)
    reduced = []
    for c, order in enumerate(orders):
        b = bufs[5 * c:5 * c + 5]
        reduced.append(Reduced(net, q, out, c * rows, unit, order, [(b[0], b[1]), (b[2], b[3]), (b[4], None)]))
        reduced[c].begin()
    for c in BEFORE:
        if c < 0:
            diag.cross()
        else:
            reduced[c].advance()
    diag.swap()
    for h in range(2):
        a[:, h * half:(h + 1) * half] = g[h].reshape(n, half)

    later = list(LATER)
    calls = [0]

    def hook():
        while later and later[0][0] <= calls[0]:
            reduced[later.pop(0)[1]].advance()
        calls[0] += 1

    factor_inverse(a, w, hook)
    wt = split(w[...].T)
    inverse = split(dot3(wt, split(w[...]), NN))

    def emit(c):
        picked = jnp.concatenate([out[c * rows + cb * tile:c * rows + (cb + 1) * tile, :] for cb in range(blocks)], axis=1)
        hi, lo = split(dot3(split(picked), inverse, NN))
        nh_ref[c * tile:(c + 1) * tile, :] = hi
        nl_ref[c * tile:(c + 1) * tile, :] = lo

    for c in range(len(orders)):
        if reduced[c].stage == 6:
            emit(c)
    for _, c in later:
        reduced[c].advance()
        if reduced[c].stage == 6:
            emit(c)
    net.drain()


def front_call(dims, orders, tile, diag, panel, tiles):
    n, cols = panel.shape[1], tiles.shape[0] * tile
    total = cols * (n // LANES)
    unit = tile * (n // LANES) // math.prod(dims)
    sems = 1 + 2 * dims[0] + 6 * len(orders)
    V = pl.BlockSpec(memory_space=pltpu.VMEM)
    return pl.pallas_call(
        functools.partial(front_kernel, dims, orders, tile),
        out_shape=(jax.ShapeDtypeStruct((cols, n), BF16),) * 2,
        in_specs=[V, pl.BlockSpec(memory_space=pl.ANY), pl.BlockSpec(memory_space=pltpu.SMEM)],
        out_specs=(V, V),
        scratch_shapes=[
            pltpu.VMEM(panel.shape, F32), pltpu.VMEM((total, LANES), F32), pltpu.VMEM((2,) + dims + (diag.shape[0], n // 2), F32),
            pltpu.VMEM((n, n), F32), pltpu.VMEM((n, n), F32), pltpu.VMEM((total, LANES), F32), pltpu.SemaphoreType.DMA,
            pltpu.SemaphoreType.DMA((sems,)), pltpu.SemaphoreType.DMA((sems,)),
        ] + scratch_for(dims, unit, orders),
        compiler_params=pltpu.CompilerParams(collective_id=0, has_side_effects=True, vmem_limit_bytes=56 << 20),
    )(diag, panel, tiles)


def update_kernel(tile, mask, p_ref, t_ref, nh_ref, nl_ref, o_ref):
    per = p_ref.shape[0] // tile
    first = pl.program_id(0) * per
    u = dot3(split(p_ref[...]), (nh_ref[...], nl_ref[...]), NT)
    for i in range(per):
        for j in range(t_ref.shape[1] // tile):
            r, c = slice(i * tile, (i + 1) * tile), slice(j * tile, (j + 1) * tile)
            t = t_ref[r, c]
            o_ref[r, c] = t - jnp.where(mask[first + i, j] != 0, u[r, c], 0.0)

def update_call(panel, trailing, mask, nh, nl, tile, rows=512):
    m, n = panel.shape
    cols = trailing.shape[1]
    whole = pl.BlockSpec((cols, n), lambda i: (0, 0))
    block = pl.BlockSpec((rows, cols), lambda i: (i, 0))
    return pl.pallas_call(functools.partial(update_kernel, tile),
        out_shape=jax.ShapeDtypeStruct(trailing.shape, F32), grid=(m // rows,),
        in_specs=[pl.BlockSpec(memory_space=pltpu.SMEM), pl.BlockSpec((rows, n), lambda i: (i, 0)), block, whole, whole],
        out_specs=block,
        compiler_params=pltpu.CompilerParams(vmem_limit_bytes=56 << 20))(mask, panel, trailing, nh, nl)


def shards(diag_block, panel, trailing, fill_mask, column_tiles):
    tile = trailing.shape[1] // column_tiles.shape[0]
    high, low = front_call(DIMS, ORDERS, tile, diag_block, panel, column_tiles)
    return update_call(panel, trailing, fill_mask, high, low, tile)


def solution(mesh):
    return jax.shard_map(
        shards,
        mesh=mesh,
        in_specs=(P("wide", None), P("wide", None), P("wide", "loop"), P("wide", "loop"), P("loop")),
        out_specs=P("wide", "loop"),
        check_vma=False,
    )
```

time: 95.5 us -> 71.8 us (0.75)
  Pallas kernels: 92.5 us -> 69.7 us
    pallas_call x1, Pallas kernels: 82.3 us -> 59.5 us  [front_call(): pl.pallas_call(functools.partial(front_kernel, dims, orders, tile), out_s...]
where the time goes in v3:
time: 71.8 us; the launch traced here: 71.1 us
  Pallas kernels  69.7 us (97%)
  local copies, waits for them, and re-layouts  1.35 us (2%)
    pallas_call x1, Pallas kernels, front_call(): pl.pallas_call(functools.partial(front_kernel, dims, orders, tile), out_s...  59.5 us
    pallas_call x1, Pallas kernels, update_call(): pl.pallas_call(functools.partial(update_kernel, tile), out_shape=jax.Shap...  10.2 us

profile of v3, /device:TPU:16, one launch (start us, length us, event | category | flops | bytes accessed | tf_op | source)
XLA Modules:
  0.0 71.1 jit_solution(6923426427075780635)
XLA Ops:
  0.0 1.4 %copy.6.mask = s32[12,8]{1,0:T(8,128)} copy(s32[12,8]{0,1:T(8,128)} %param.8) | data formatting | bytes 768 | tf_op args[3]
  1.4 59.5 %shard_map.55 = (bf16[1024,512]{1,0:T(8,128)(2,1)}, bf16[1024,512]{1,0:T(8,128)(2,1)}) custom-call(f32[8,512]{1,0:T(8,128)} %d_ref.1, f32[1536,512]{1,0:T(8,128)} %p_ref.1, s32[8]{0:T(128)} %tiles.1), custom_call_target="tpu_custom_call" | custom-call | tf_op jit(solution)/shard_map/pallas_call | solution.py:351
  60.9 10.2 %shard_map.56 = f32[1536,1024]{1,0:T(8,128)} custom-call(s32[12,8]{1,0:T(8,128)} %copy.6.mask, f32[1536,512]{1,0:T(8,128)} %p_ref.1, f32[1536,1024]{1,0:T(8,128)} %t_ref.1, bf16[1024,512]{1,0:T(8,128)(2,1)} %get-tuple-element.7.nh_ref, bf16[1024,512]{1,0:T(8,128)(2,1)} %get-tuple-element.8.nl_ref), custom_call_target="tpu_custom_call" | custom-call | tf_op jit(solution)/shard_map/pallas_call | solution.py:380

commit v4 on v3

--- a/solution.py
+++ b/solution.py
@@ -15,6 +15,7 @@
 NT = (((1,), (1,)), ((), ()))
 NN = (((1,), (0,)), ((), ()))
 DIMS = (4, 8, 2)
+FRONT_VMEM, UPDATE_VMEM = 28 << 20, 24 << 20
 ORDERS = (
     (0, 2, 1),
     (2, 0, 1),
@@ -283,13 +284,15 @@
     lax.fori_loop(0, tile // SUB, step, 0)
 
 
-def front_kernel(dims, orders, tile, d_ref, panel_hbm, tiles, nh_ref, nl_ref, panel, q, g, a, w, out, local, send, recv, *bufs):
+def front_kernel(dims, orders, tile, d_ref, panel_hbm, t_in, tiles, nh_ref, nl_ref, ph_ref, pl_ref, t_out, panel, q, g, a, w, out, local, send, recv, *bufs):
     n = a.shape[0]
     blocks = n // LANES
     half = n // 2
     net = Net(dims, send, recv)
-    load = pltpu.make_async_copy(panel_hbm, panel, local)
+    load = pltpu.make_async_copy(panel_hbm, panel, local.at[0])
     load.start()
+    hand = pltpu.make_async_copy(t_in, t_out, local.at[1])
+    hand.start()
     greeted = net.greet()
     g[net.core, net.me[0], net.me[1], net.me[2]] = d_ref[:, pl.ds(pl.multiple_of(net.core * half, LANES), half)]
     load.wait()
@@ -310,6 +313,13 @@
             diag.cross()
         else:
             reduced[c].advance()
+
+    def parts(r, carry):
+        rows = pl.ds(pl.multiple_of(r * tile, tile), tile)
+        ph_ref[rows, :], pl_ref[rows, :] = split(panel[rows, :])
+        return carry
+
+    lax.fori_loop(0, panel.shape[0] // tile, parts, 0)
     diag.swap()
     for h in range(2):
         a[:, h * half:(h + 1) * half] = g[h].reshape(n, half)
@@ -326,68 +336,88 @@
     wt = split(w[...].T)
     inverse = split(dot3(wt, split(w[...]), NN))
 
-    def emit(c):
-        picked = jnp.concatenate([out[c * rows + cb * tile:c * rows + (cb + 1) * tile, :] for cb in range(blocks)], axis=1)
-        hi, lo = split(dot3(split(picked), inverse, NN))
-        nh_ref[c * tile:(c + 1) * tile, :] = hi
-        nl_ref[c * tile:(c + 1) * tile, :] = lo
-
-    for c in range(len(orders)):
-        if reduced[c].stage == 6:
-            emit(c)
+    def emit(group):
+        picked = [jnp.concatenate([out[c * rows + cb * tile:c * rows + (cb + 1) * tile, :] for cb in range(blocks)], axis=1) for c in group]
+        hi, lo = split(dot3(split(jnp.concatenate(picked, axis=0)), inverse, NN))
+        for i, c in enumerate(group):
+            nh_ref[c * tile:(c + 1) * tile, :] = hi[i * tile:(i + 1) * tile]
+            nl_ref[c * tile:(c + 1) * tile, :] = lo[i * tile:(i + 1) * tile]
+
+    ended = [c for c in range(len(orders)) if reduced[c].stage == 6]
     for _, c in later:
+        if len(ended) >= 2:
+            emit(ended)
+            ended = []
         reduced[c].advance()
         if reduced[c].stage == 6:
-            emit(c)
+            ended.append(c)
+    emit(ended)
+    hand.wait()
     net.drain()
 
 
-def front_call(dims, orders, tile, diag, panel, tiles):
+def front_call(dims, orders, tile, diag, panel, trailing, tiles):
     n, cols = panel.shape[1], tiles.shape[0] * tile
     total = cols * (n // LANES)
     unit = tile * (n // LANES) // math.prod(dims)
     sems = 1 + 2 * dims[0] + 6 * len(orders)
     V = pl.BlockSpec(memory_space=pltpu.VMEM)
+    A = pl.BlockSpec(memory_space=pl.ANY)
+    H = pl.BlockSpec(memory_space=pltpu.HBM)
     return pl.pallas_call(
         functools.partial(front_kernel, dims, orders, tile),
-        out_shape=(jax.ShapeDtypeStruct((cols, n), BF16),) * 2,
-        in_specs=[V, pl.BlockSpec(memory_space=pl.ANY), pl.BlockSpec(memory_space=pltpu.SMEM)],
-        out_specs=(V, V),
+        out_shape=(jax.ShapeDtypeStruct((cols, n), BF16),) * 2 + (jax.ShapeDtypeStruct(panel.shape, BF16),) * 2 + (jax.ShapeDtypeStruct(trailing.shape, F32),),
+        in_specs=[V, H, H, pl.BlockSpec(memory_space=pltpu.SMEM)],
+        out_specs=(V, V, V, V, A),
         scratch_shapes=[
             pltpu.VMEM(panel.shape, F32), pltpu.VMEM((total, LANES), F32), pltpu.VMEM((2,) + dims + (diag.shape[0], n // 2), F32),
-            pltpu.VMEM((n, n), F32), pltpu.VMEM((n, n), F32), pltpu.VMEM((total, LANES), F32), pltpu.SemaphoreType.DMA,
+            pltpu.VMEM((n, n), F32), pltpu.VMEM((n, n), F32), pltpu.VMEM((total, LANES), F32), pltpu.SemaphoreType.DMA((2,)),
             pltpu.SemaphoreType.DMA((sems,)), pltpu.SemaphoreType.DMA((sems,)),
         ] + scratch_for(dims, unit, orders),
-        compiler_params=pltpu.CompilerParams(collective_id=0, has_side_effects=True, vmem_limit_bytes=56 << 20),
-    )(diag, panel, tiles)
-
-
-def update_kernel(tile, mask, p_ref, t_ref, nh_ref, nl_ref, o_ref):
-    per = p_ref.shape[0] // tile
-    first = pl.program_id(0) * per
-    u = dot3(split(p_ref[...]), (nh_ref[...], nl_ref[...]), NT)
-    for i in range(per):
-        for j in range(t_ref.shape[1] // tile):
-            r, c = slice(i * tile, (i + 1) * tile), slice(j * tile, (j + 1) * tile)
-            t = t_ref[r, c]
-            o_ref[r, c] = t - jnp.where(mask[first + i, j] != 0, u[r, c], 0.0)
-
-def update_call(panel, trailing, mask, nh, nl, tile, rows=512):
-    m, n = panel.shape
-    cols = trailing.shape[1]
-    whole = pl.BlockSpec((cols, n), lambda i: (0, 0))
-    block = pl.BlockSpec((rows, cols), lambda i: (i, 0))
-    return pl.pallas_call(functools.partial(update_kernel, tile),
-        out_shape=jax.ShapeDtypeStruct(trailing.shape, F32), grid=(m // rows,),
-        in_specs=[pl.BlockSpec(memory_space=pltpu.SMEM), pl.BlockSpec((rows, n), lambda i: (i, 0)), block, whole, whole],
-        out_specs=block,
-        compiler_params=pltpu.CompilerParams(vmem_limit_bytes=56 << 20))(mask, panel, trailing, nh, nl)
+        cost_estimate=pl.CostEstimate(flops=10 * n**3, bytes_accessed=200_000_000, transcendentals=0),
+        compiler_params=pltpu.CompilerParams(collective_id=0, has_side_effects=True, vmem_limit_bytes=FRONT_VMEM),
+    )(diag, panel, trailing, tiles)
+
+
+def update_kernel(tile, rows, mask, ph_ref, pl_ref, t_ref, nh_ref, nl_ref, o_hbm, o, sems):
+    steps = t_ref.shape[0] // rows
+
+    def part(k):
+        return pl.ds(pl.multiple_of(k * rows, rows), rows)
+
+    def step(k, carry):
+        u = dot3((ph_ref[part(k), :], pl_ref[part(k), :]), (nh_ref[...], nl_ref[...]), NT)
+        for i in range(rows // tile):
+            r = pl.ds(pl.multiple_of(k * rows + i * tile, tile), tile)
+            for j in range(t_ref.shape[1] // tile):
+                c = slice(j * tile, (j + 1) * tile)
+                filled = mask[j, k * (rows // tile) + i] != 0
+                o[r, c] = t_ref[r, c] - jnp.where(filled, u[i * tile:(i + 1) * tile, c], 0.0)
+        pltpu.make_async_copy(o.at[part(k)], o_hbm.at[part(k)], sems.at[k]).start()
+        return carry
+
+    lax.fori_loop(0, steps, step, 0)
+    for k in range(steps):
+        pltpu.make_async_copy(o.at[part(k)], o_hbm.at[part(k)], sems.at[k]).wait()
+
+
+def update_call(ph, pl_, trailing, mask, nh, nl, tile, rows=512):
+    V = pl.BlockSpec(memory_space=pltpu.VMEM)
+    return pl.pallas_call(
+        functools.partial(update_kernel, tile, rows),
+        out_shape=jax.ShapeDtypeStruct(trailing.shape, F32),
+        in_specs=[pl.BlockSpec(memory_space=pltpu.SMEM), V, V, V, V, V],
+        out_specs=pl.BlockSpec(memory_space=pl.ANY),
+        scratch_shapes=[pltpu.VMEM(trailing.shape, F32), pltpu.SemaphoreType.DMA((trailing.shape[0] // rows,))],
+        compiler_params=pltpu.CompilerParams(vmem_limit_bytes=UPDATE_VMEM),
+    )(mask, ph, pl_, trailing, nh, nl)
 
 
 def shards(diag_block, panel, trailing, fill_mask, column_tiles):
     tile = trailing.shape[1] // column_tiles.shape[0]
-    high, low = front_call(DIMS, ORDERS, tile, diag_block, panel, column_tiles)
-    return update_call(panel, trailing, fill_mask, high, low, tile)
+    far = [pltpu.with_memory_space_constraint(x, pltpu.HBM) for x in (diag_block, panel, trailing, column_tiles)]
+    high, low, panel_high, panel_low, kept = front_call(DIMS, ORDERS, tile, *far)
+    return update_call(panel_high, panel_low, kept, fill_mask.T, high, low, tile)
 
 
 def solution(mesh):

time: 71.8 us -> 66.3 us (0.923)
  Pallas kernels: 69.7 us -> 65.5 us
  local copies, waits for them, and re-layouts: 1.35 us -> 0.01 us
    pallas_call x1, Pallas kernels: 10.2 us -> 7.57 us  [update_call(): pl.pallas_call(functools.partial(update_kernel, tile, rows), out_shape=ja...]
    pallas_call x1, Pallas kernels: 59.5 us -> 58 us  [front_call(): pl.pallas_call(functools.partial(front_kernel, dims, orders, tile), out_s...]
    unnamed x1 -> x2, local copies, waits for them, and re-layouts: 1.35 us -> 0.01 us
where the time goes in v4:
time: 66.3 us; the launch traced here: 65.7 us
  Pallas kernels  65.5 us (99%)
    pallas_call x1, Pallas kernels, front_call(): pl.pallas_call(functools.partial(front_kernel, dims, orders, tile), out_s...  58 us
    pallas_call x1, Pallas kernels, update_call(): pl.pallas_call(functools.partial(update_kernel, tile, rows), out_shape=ja...  7.57 us

profile of v4, /device:TPU:16, one launch (start us, length us, event | category | flops | bytes accessed | tf_op | source)
XLA Modules:
  0.0 65.7 jit_solution(12264013260150025667)
XLA Ops:
  0.0 0.0 copy-start
  0.0 58.0 %shard_map.55 = (bf16[1024,512]{1,0:T(8,128)(2,1)S(1)}, bf16[1024,512]{1,0:T(8,128)(2,1)S(1)}, bf16[1536,512]{1,0:T(8,128)(2,1)S(1)}, bf16[1536,512]{1,0:T(8,128)(2,1)S(1)}, f32[1536,1024]{1,0:T(8,128)S(1)}) custom-call(f32[8,512]{1,0:T(8,128)} %d_ref.1, f32[1536,512]{1,0:T(8,128)} %panel_hbm.1, f32[1536,1024]{1,0:T(8,128)} %t_in.1, s32[8]{0:T(128)} %tiles.1), custom_call_target="tpu_custom_call" | custom-call | flops 1342177280 | bytes 200000000 | tf_op jit(solution)/shard_map/pallas_call | solution.py:367
  58.0 0.0 copy-done
  58.0 7.6 %shard_map.56 = f32[1536,1024]{1,0:T(8,128)} custom-call(s32[8,12]{1,0:T(8,128)S(1)} %bitcast.1, bf16[1536,512]{1,0:T(8,128)(2,1)S(1)} %get-tuple-element.10.ph_ref, bf16[1536,512]{1,0:T(8,128)(2,1)S(1)} %get-tuple-element.11.pl_ref, f32[1536,1024]{1,0:T(8,128)S(1)} %get-tuple-element.12.t_ref, bf16[1024,512]{1,0:T(8,128)(2,1)S(1)} %get-tuple-element.13.nh_ref, ...), custom_call_target="tpu_custom_call" | custom-call | tf_op jit(solution)/shard_map/pallas_call | solution.py:406
Async XLA Ops:
  0.0 58.0 %copy-start = (s32[12,8]{0,1:T(8,128)S(1)}, s32[12,8]{0,1:T(8,128)}, u32[]{:S(2)}) copy-start(s32[12,8]{0,1:T(8,128)} %param.8) | copy-start | bytes 1156

commit v5 on v4

--- a/solution.py
+++ b/solution.py
@@ -22,19 +22,19 @@
     (2, 0, 1),
     (1, 0, 2),
     (0, 2, 1),
+    (2, 0, 1),
     (1, 0, 2),
     (2, 0, 1),
-    (2, 0, 1),
 )
-BEFORE = (1, 0, -1, 2, 4, 1, 3, 6)
+BEFORE = (1, 0, -1, 2, 4, 1, 3, 5)
 LATER = (
-    (0, 7), (0, 2), (0, 0), (0, 3), (0, 4), (3, 6), (3, 5), (5, 1),
-    (7, 3), (9, 7), (10, 2), (12, 0), (13, 5), (14, 4), (14, 3), (16, 6),
-    (18, 1), (21, 5), (21, 7), (23, 2), (24, 3), (25, 0), (27, 4), (29, 5),
-    (29, 6), (30, 1), (34, 7), (35, 0), (36, 2), (37, 4), (38, 5), (42, 6),
-    (46, 1), (46, 7), (50, 3), (53, 2), (54, 0), (61, 6), (61, 4), (65, 5),
-    (69, 7),
+    (0, 7), (0, 2), (0, 0), (0, 3), (0, 4), (3, 5), (3, 6), (5, 1),
+    (7, 3), (9, 7), (10, 2), (12, 0), (13, 6), (14, 4), (14, 3), (16, 5),
+    (18, 1), (21, 6), (21, 7), (23, 2), (24, 3), (25, 0), (27, 4), (29, 6),
+    (29, 5), (30, 1), (34, 7), (35, 0), (36, 2), (37, 4), (38, 6), (42, 5),
+    (46, 7),
 )
+GROUPS = ((1, 3, 2, 0), (5, 4), (6, 7))
 
 
 def lane_bcast(x, lane):
@@ -57,8 +57,12 @@
         own = jnp.where(here, jnp.where(lane - base == sub, 1.0, 0.0), own)
         invs, tops, edges = [], [], {}
         scale = jnp.ones((SUB, WIDE), F32)
+        pivot = sub_bcast(cols[0], 0)
         for p in range(SUB):
-            inv = 1.0 / sub_bcast(cols[p], p)
+            inv = 1.0 / pivot
+            if p < SUB - 1:
+                edges[p, p + 1] = sub_bcast(cols[p + 1], p)
+                pivot = sub_bcast(cols[p + 1], p + 1) - (sub_bcast(cols[p], p + 1) * inv) * edges[p, p + 1]
             invs.append(inv)
             scale = jnp.where(sub == p, inv, scale)
             top = sub_bcast(own, p)
@@ -66,7 +70,8 @@
             if p < SUB - 1:
                 mult = jnp.where(sub > p, cols[p] * inv, 0.0)
                 for q in range(p + 1, SUB):
-                    edges[p, q] = sub_bcast(cols[q], p)
+                    if q > p + 1:
+                        edges[p, q] = sub_bcast(cols[q], p)
                     cols[q] = cols[q] - mult * edges[p, q]
                 own = own - mult * top
         rows[k] = own
@@ -83,33 +88,76 @@
         hook()
     return rows, scales
 
+def exact(x, y, dims=NN):
+    return lax.dot_general(x, y, dims, precision=HI, preferred_element_type=F32)
+
+
 def factor_inverse(a, w, hook):
     n = a.shape[0]
     tiles = n // WIDE
     lane = lax.broadcasted_iota(jnp.int32, (WIDE, WIDE), 1)
     sub = lax.broadcasted_iota(jnp.int32, (WIDE, WIDE), 0)
     w[...] = jnp.zeros_like(w)
+    waiting = []
+
+    def between():
+        if waiting:
+            waiting.pop(0)()
+        hook()
+
+    def less(rows, cols, x, y):
+        a[rows, cols] = a[rows, cols] - exact(x, y)
+
     for j in range(tiles):
-        lo, hi = j * WIDE, (j + 1) * WIDE
-        rows = [a[lo + SUB * k: lo + SUB * (k + 1), lo:hi] for k in range(WIDE // SUB)]
-        rows, scales = factor_tile(rows, hook)
+        own = slice(j * WIDE, (j + 1) * WIDE)
+        rows = [a[j * WIDE + SUB * k:j * WIDE + SUB * (k + 1), own] for k in range(WIDE // SUB)]
+        rows, scales = factor_tile(rows, between)
+        assert not waiting
         linv = jnp.where(lane <= sub, jnp.concatenate(rows, axis=0), 0.0)
         inv = jnp.concatenate(scales, axis=0)
         root = jnp.sqrt(inv)
-        w[lo:hi, lo:hi] = linv * root
-        if j + 1 < tiles:
-            right = jnp.dot(linv, a[lo:hi, hi:], precision=HI, preferred_element_type=F32)
-            mult = lax.dot_general(a[hi:, lo:hi], linv, NT, precision=HI, preferred_element_type=F32)
-        if j:
-            left = jnp.dot(linv, a[lo:hi, :lo], precision=HI, preferred_element_type=F32)
-            w[lo:hi, :lo] = left * jnp.concatenate([root] * j, axis=1)
-        if j + 1 < tiles:
-            scaled = right * jnp.concatenate([inv] * (tiles - 1 - j), axis=1)
-            a[hi:, hi:] = a[hi:, hi:] - jnp.dot(mult, scaled, precision=HI, preferred_element_type=F32)
-            a[hi:, lo:hi] = -jnp.dot(mult, linv * inv, precision=HI, preferred_element_type=F32)
-            if j:
-                scaled = left * jnp.concatenate([inv] * j, axis=1)
-                a[hi:, :lo] = a[hi:, :lo] - jnp.dot(mult, scaled, precision=HI, preferred_element_type=F32)
+        w[own, own] = linv * root
+        if j + 1 == tiles:
+            for i in range(j):
+                at = slice(i * WIDE, (i + 1) * WIDE)
+                w[own, at] = exact(linv, a[own, at]) * root
+            break
+        right, mult = {}, {}
+        for i in range(j + 1, tiles):
+            at = slice(i * WIDE, (i + 1) * WIDE)
+            right[i] = a[own, at]
+            mult[i] = a[at, own]
+
+        def solve(i, linv=linv, inv=inv, right=right, mult=mult):
+            right[i] = exact(linv, right[i]) * inv
+            mult[i] = exact(mult[i], linv, NT)
+
+        solve(j + 1)
+        after = slice((j + 1) * WIDE, (j + 2) * WIDE)
+        less(after, after, mult[j + 1], right[j + 1])
+
+        for i in range(j + 2, tiles):
+            waiting.append(functools.partial(solve, i))
+
+        def update(i, j=j, own=own, linv=linv, inv=inv, right=right, mult=mult):
+            at = slice(i * WIDE, (i + 1) * WIDE)
+            for c in range(j + 1, tiles):
+                if (i, c) != (j + 1, j + 1):
+                    less(at, slice(c * WIDE, (c + 1) * WIDE), mult[i], right[c])
+            a[at, own] = -exact(mult[i], linv * inv)
+
+        def finish(c, j=j, own=own, linv=linv, inv=inv, root=root, mult=mult):
+            at = slice(c * WIDE, (c + 1) * WIDE)
+            left = exact(linv, a[own, at])
+            w[own, at] = left * root
+            left = left * inv
+            for i in range(j + 1, tiles):
+                less(slice(i * WIDE, (i + 1) * WIDE), at, mult[i], left)
+
+        for i in range(j + 1, tiles):
+            waiting.append(functools.partial(update, i))
+        for c in range(j):
+            waiting.append(functools.partial(finish, c))
 
 
 class Net:
@@ -122,14 +170,17 @@
         self.core = lax.rem(loop, 2)
         self.twin = {"loop": loop + 1 - 2 * self.core}
         self.send, self.recv, self.used, self.sent = send, recv, 0, []
+        self.known = {}
 
     def peer(self, steps):
         c = [lax.rem(c + s, n) for c, s, n in zip(self.me, steps, self.dims)]
         return c, {"wide": (c[0] * self.dims[1] + c[1]) * self.dims[2] + c[2]}
 
     def along(self, axis, step):
-        c, device = self.peer([step if a == axis else 0 for a in range(3)])
-        return c[axis], device
+        if (axis, step) not in self.known:
+            c, device = self.peer([step if a == axis else 0 for a in range(3)])
+            self.known[axis, step] = c[axis], device
+        return self.known[axis, step]
 
     def plane(self):
         steps = [(0, dz, dy) for dz in range(self.dims[1]) for dy in range(self.dims[2]) if dz or dy]
@@ -284,7 +335,7 @@
     lax.fori_loop(0, tile // SUB, step, 0)
 
 
-def front_kernel(dims, orders, tile, d_ref, panel_hbm, t_in, tiles, nh_ref, nl_ref, ph_ref, pl_ref, t_out, panel, q, g, a, w, out, local, send, recv, *bufs):
+def front_kernel(dims, orders, groups, tile, d_ref, panel_hbm, t_in, tiles, mask, nh_ref, nl_ref, ph_ref, pl_ref, t_out, panel, q, g, a, w, out, local, send, recv, *bufs):
     n = a.shape[0]
     blocks = n // LANES
     half = n // 2
@@ -343,32 +394,30 @@
             nh_ref[c * tile:(c + 1) * tile, :] = hi[i * tile:(i + 1) * tile]
             nl_ref[c * tile:(c + 1) * tile, :] = lo[i * tile:(i + 1) * tile]
 
-    ended = [c for c in range(len(orders)) if reduced[c].stage == 6]
-    for _, c in later:
-        if len(ended) >= 2:
-            emit(ended)
-            ended = []
-        reduced[c].advance()
-        if reduced[c].stage == 6:
-            ended.append(c)
-    emit(ended)
-    hand.wait()
+    for k, group in enumerate(groups):
+        for c in group:
+            reduced[c].advance()
+        group = sorted(group)
+        emit(group)
+        if k == 0:
+            hand.wait()
+        if k < len(groups) - 1:
+            update_columns(tile, mask, group[0], len(group), ph_ref, pl_ref, nh_ref, nl_ref, t_out, t_out, lambda r: None)
     net.drain()
 
 
-def front_call(dims, orders, tile, diag, panel, trailing, tiles):
+def front_call(dims, orders, groups, tile, diag, panel, trailing, tiles, mask):
     n, cols = panel.shape[1], tiles.shape[0] * tile
     total = cols * (n // LANES)
     unit = tile * (n // LANES) // math.prod(dims)
     sems = 1 + 2 * dims[0] + 6 * len(orders)
     V = pl.BlockSpec(memory_space=pltpu.VMEM)
-    A = pl.BlockSpec(memory_space=pl.ANY)
     H = pl.BlockSpec(memory_space=pltpu.HBM)
     return pl.pallas_call(
-        functools.partial(front_kernel, dims, orders, tile),
+        functools.partial(front_kernel, dims, orders, groups, tile),
         out_shape=(jax.ShapeDtypeStruct((cols, n), BF16),) * 2 + (jax.ShapeDtypeStruct(panel.shape, BF16),) * 2 + (jax.ShapeDtypeStruct(trailing.shape, F32),),
-        in_specs=[V, H, H, pl.BlockSpec(memory_space=pltpu.SMEM)],
-        out_specs=(V, V, V, V, A),
+        in_specs=[V, H, H] + [pl.BlockSpec(memory_space=pltpu.SMEM)] * 2,
+        out_specs=(V,) * 5,
         scratch_shapes=[
             pltpu.VMEM(panel.shape, F32), pltpu.VMEM((total, LANES), F32), pltpu.VMEM((2,) + dims + (diag.shape[0], n // 2), F32),
             pltpu.VMEM((n, n), F32), pltpu.VMEM((n, n), F32), pltpu.VMEM((total, LANES), F32), pltpu.SemaphoreType.DMA((2,)),
@@ -376,48 +425,62 @@
         ] + scratch_for(dims, unit, orders),
         cost_estimate=pl.CostEstimate(flops=10 * n**3, bytes_accessed=200_000_000, transcendentals=0),
         compiler_params=pltpu.CompilerParams(collective_id=0, has_side_effects=True, vmem_limit_bytes=FRONT_VMEM),
-    )(diag, panel, trailing, tiles)
-
-
-def update_kernel(tile, rows, mask, ph_ref, pl_ref, t_ref, nh_ref, nl_ref, o_hbm, o, sems):
-    steps = t_ref.shape[0] // rows
-
-    def part(k):
-        return pl.ds(pl.multiple_of(k * rows, rows), rows)
-
-    def step(k, carry):
-        u = dot3((ph_ref[part(k), :], pl_ref[part(k), :]), (nh_ref[...], nl_ref[...]), NT)
+    )(diag, panel, trailing, tiles, mask)
+
+
+def update_columns(tile, mask, first, count, ph_ref, pl_ref, nh_ref, nl_ref, t_ref, o_ref, after):
+    rows = 4 * tile
+    cols = slice(first * tile, (first + count) * tile)
+
+    def step(r, carry):
+        part = pl.ds(pl.multiple_of(r * rows, rows), rows)
+        u = dot3((ph_ref[part, :], pl_ref[part, :]), (nh_ref[cols, :], nl_ref[cols, :]), NT)
         for i in range(rows // tile):
-            r = pl.ds(pl.multiple_of(k * rows + i * tile, tile), tile)
-            for j in range(t_ref.shape[1] // tile):
-                c = slice(j * tile, (j + 1) * tile)
-                filled = mask[j, k * (rows // tile) + i] != 0
-                o[r, c] = t_ref[r, c] - jnp.where(filled, u[i * tile:(i + 1) * tile, c], 0.0)
-        pltpu.make_async_copy(o.at[part(k)], o_hbm.at[part(k)], sems.at[k]).start()
+            at = pl.ds(pl.multiple_of(r * rows + i * tile, tile), tile)
+            for j in range(count):
+                c = slice((first + j) * tile, (first + j + 1) * tile)
+                filled = jnp.full((tile, tile), mask[first + j, r * (rows // tile) + i], jnp.int32) != 0
+                o_ref[at, c] = t_ref[at, c] - jnp.where(filled, u[i * tile:(i + 1) * tile, j * tile:(j + 1) * tile], 0.0)
+        after(r)
         return carry
 
-    lax.fori_loop(0, steps, step, 0)
-    for k in range(steps):
-        pltpu.make_async_copy(o.at[part(k)], o_hbm.at[part(k)], sems.at[k]).wait()
-
-
-def update_call(ph, pl_, trailing, mask, nh, nl, tile, rows=512):
+    lax.fori_loop(0, t_ref.shape[0] // rows, step, 0)
+
+
+def update_kernel(tile, first, mask, ph_ref, pl_ref, t_ref, nh_ref, nl_ref, o_hbm, o, sems):
+    steps = t_ref.shape[0] // (4 * tile)
+    edge = first * tile
+
+    def write(r, ref, cols, k):
+        rows = pl.ds(pl.multiple_of(r * 4 * tile, 4 * tile), 4 * tile)
+        return pltpu.make_async_copy(ref.at[rows, cols], o_hbm.at[rows, cols], sems.at[k, r])
+
+    done, rest = slice(0, edge), slice(edge, t_ref.shape[1])
+    for r in range(steps):
+        write(r, t_ref, done, 0).start()
+    update_columns(tile, mask, first, mask.shape[0] - first, ph_ref, pl_ref, nh_ref, nl_ref, t_ref, o, lambda r: write(r, o, rest, 1).start())
+    for r in range(steps):
+        write(r, t_ref, done, 0).wait()
+        write(r, o, rest, 1).wait()
+
+
+def update_call(ph, pl_, trailing, mask, nh, nl, tile, first):
     V = pl.BlockSpec(memory_space=pltpu.VMEM)
     return pl.pallas_call(
-        functools.partial(update_kernel, tile, rows),
+        functools.partial(update_kernel, tile, first),
         out_shape=jax.ShapeDtypeStruct(trailing.shape, F32),
         in_specs=[pl.BlockSpec(memory_space=pltpu.SMEM), V, V, V, V, V],
         out_specs=pl.BlockSpec(memory_space=pl.ANY),
-        scratch_shapes=[pltpu.VMEM(trailing.shape, F32), pltpu.SemaphoreType.DMA((trailing.shape[0] // rows,))],
+        scratch_shapes=[pltpu.VMEM(trailing.shape, F32), pltpu.SemaphoreType.DMA((2, trailing.shape[0] // (4 * tile)))],
         compiler_params=pltpu.CompilerParams(vmem_limit_bytes=UPDATE_VMEM),
     )(mask, ph, pl_, trailing, nh, nl)
 
 
 def shards(diag_block, panel, trailing, fill_mask, column_tiles):
     tile = trailing.shape[1] // column_tiles.shape[0]
-    far = [pltpu.with_memory_space_constraint(x, pltpu.HBM) for x in (diag_block, panel, trailing, column_tiles)]
-    high, low, panel_high, panel_low, kept = front_call(DIMS, ORDERS, tile, *far)
-    return update_call(panel_high, panel_low, kept, fill_mask.T, high, low, tile)
+    far = [pltpu.with_memory_space_constraint(x, pltpu.HBM) for x in (diag_block, panel, trailing, column_tiles, fill_mask.T)]
+    high, low, panel_high, panel_low, kept = front_call(DIMS, ORDERS, GROUPS, tile, *far)
+    return update_call(panel_high, panel_low, kept, far[4], high, low, tile, min(GROUPS[-1]))
 
 
 def solution(mesh):

time: 66.3 us -> 65.7 us (level)
  no operation moved by 1% of the time
where the time goes in v5:
time: 65.7 us; the launch traced here: 65 us
  Pallas kernels  64.9 us (99%)
    pallas_call x1, Pallas kernels, front_call(): pl.pallas_call(functools.partial(front_kernel, dims, orders, groups, tile...  61.4 us
    pallas_call x1, Pallas kernels, update_call(): pl.pallas_call(functools.partial(update_kernel, tile, first), out_shape=j...  3.44 us

profile of v5, /device:TPU:16, one launch (start us, length us, event | category | flops | bytes accessed | tf_op | source)
XLA Modules:
  0.0 65.0 jit_solution(11697945058956130811)
XLA Ops:
  0.0 61.4 %shard_map.55 = (bf16[1024,512]{1,0:T(8,128)(2,1)S(1)}, bf16[1024,512]{1,0:T(8,128)(2,1)S(1)}, bf16[1536,512]{1,0:T(8,128)(2,1)S(1)}, bf16[1536,512]{1,0:T(8,128)(2,1)S(1)}, f32[1536,1024]{1,0:T(8,128)S(1)}) custom-call(f32[8,512]{1,0:T(8,128)} %d_ref.1, f32[1536,512]{1,0:T(8,128)} %panel_hbm.1, f32[1536,1024]{1,0:T(8,128)} %t_in.1, s32[8]{0:T(128)} %tiles.1, ...), custom_call_target="tpu_custom_call" | custom-call | flops 1342177280 | bytes 200000000 | tf_op jit(solution)/shard_map/pallas_call | solution.py:416
  61.4 3.4 %shard_map.56 = f32[1536,1024]{1,0:T(8,128)} custom-call(s32[8,12]{1,0:T(8,128)} %bitcast.2, bf16[1536,512]{1,0:T(8,128)(2,1)S(1)} %get-tuple-element.10.ph_ref, bf16[1536,512]{1,0:T(8,128)(2,1)S(1)} %get-tuple-element.11.pl_ref, f32[1536,1024]{1,0:T(8,128)S(1)} %get-tuple-element.12.t_ref, bf16[1024,512]{1,0:T(8,128)(2,1)S(1)} %get-tuple-element.13.nh_ref, ...), custom_call_target="tpu_custom_call" | custom-call | tf_op jit(solution)/shard_map/pallas_call | solution.py:469
